TPU v7x, 256 devices: a whole 4x4x8 slice. The times are simulated.
256 devices in a mesh: seq: 16 (over z, x_lo), wt: 16 (over x_hi, y, core).
Axes of the slice: x: 4 (x_hi: 2, x_lo: 2; x = x_hi * 2 + x_lo), y: 4, z: 8, core: 2. Of those that a mesh axis runs over, the one named last changes fastest.
Arguments:
- frames: bfloat16 [4096, 4096], P('seq'), may hold values from -40 to 40
- attn_norm_gain: float32 [4096], replicated, may hold values from 0.1 to 1.9
- qkv_weight: bfloat16 [3, 4096, 4096], P(None, 'seq', 'wt'), may hold values from -4 to 4
- attn_out_weight: bfloat16 [4096, 4096], P('seq', 'wt'), may hold values from -0.125 to 0.125
- conv_norm_gain: float32 [4096], replicated, may hold values from 0.1 to 1.9
- glu_weight: bfloat16 [2, 4096, 4096], P(None, 'seq', 'wt'), may hold values from -0.09375 to 0.09375
- depth_kernel: float32 [31, 4096], P(None, 'wt'), may hold values from -1 to 1
- norm_scale: float32 [4096], P('wt'), may hold values from 0.5 to 2
- norm_shift: float32 [4096], P('wt'), may hold values from -3 to 3
- conv_out_weight: bfloat16 [4096, 4096], P('seq', 'wt'), may hold values from -0.125 to 0.125
Outputs:
- encoded: bfloat16 [4096, 4096], P('seq', 'wt')
All inputs are finite; a program needn't handle non-finite values.
Results may differ from a plain program's by a relative error of at most 0.014.
Values may be sent and summed in bfloat16 or wider, within the bound.
No kernel may reach another device: no remote copies, remote signals or barrier semaphores. Data moves between devices by JAX's collectives and lax.ppermute only.
A program may use at most 64 MiB of HBM per device.

v0:
```python
import jax
import jax.numpy as jnp
from jax import lax
from jax.sharding import PartitionSpec as P

HEAD_DIM = 128


def padded_2(value, sides, width):
    for axis, dim in sides:
        devices, length = (lax.axis_size(axis), value.shape[dim])
        up = [(i, (i + 1) % devices) for i in range(devices - 1)]
        down = [(j, i) for i, j in up]
        last = lax.slice_in_dim(value, length - width, length, axis=dim)
        first = lax.slice_in_dim(value, 0, width, axis=dim)
        before = lax.ppermute(last, axis, up)
        after = lax.ppermute(first, axis, down)
        value = jnp.concatenate([before, value, after], axis=dim)
    return value


def norm_rows(values, gain_vec):
    wide = values.astype(jnp.float32)
    row_mean = jnp.mean(wide, axis=-1, keepdims=True)
    centered = wide - row_mean
    row_var = jnp.mean(centered * centered, axis=-1, keepdims=True)
    return (centered * lax.rsqrt(row_var + 1e-05) * gain_vec).astype(jnp.bfloat16)


def project_in(normed, stacked):
    return jnp.einsum(
        "rd,mdc->rmc",
        normed,
        lax.all_gather(stacked, "seq", axis=1, tiled=True),
        preferred_element_type=jnp.float32,
    )


def project_out(inputs, weight):
    return lax.dot_general(
        inputs,
        lax.all_gather(weight, "seq", axis=0, tiled=True),
        (((1,), (1,)), ((), ())),
        preferred_element_type=jnp.float32,
    )


def feature_share(partial_sums):
    return lax.psum_scatter(
        partial_sums.astype(jnp.bfloat16), "wt", scatter_dimension=1, tiled=True
    ).astype(jnp.float32)


def local(
    frames,
    attn_norm_gain,
    qkv_weight,
    attn_out_weight,
    conv_norm_gain,
    glu_weight,
    depth_kernel,
    norm_scale,
    norm_shift,
    conv_out_weight,
):
    row_count = frames.shape[0]
    col_count = qkv_weight.shape[2]
    heads_here = col_count // HEAD_DIM
    column_start = lax.axis_index("wt") * col_count
    normed = norm_rows(frames, attn_norm_gain)
    projected = project_in(normed, qkv_weight).astype(jnp.bfloat16)
    query_heads = projected[:, 0].reshape(row_count, heads_here, HEAD_DIM)
    keys = projected[:, 1]
    values = projected[:, 2]
    score_scale = HEAD_DIM ** (-0.5)
    key_segment = lax.all_gather(keys, "seq", axis=0, tiled=True)
    value_segment = lax.all_gather(values, "seq", axis=0, tiled=True)
    row_best = jnp.full((heads_here, row_count), -1e30, jnp.float32)
    key_heads = key_segment.reshape(key_segment.shape[0], heads_here, HEAD_DIM)
    value_heads = value_segment.reshape(value_segment.shape[0], heads_here, HEAD_DIM)
    scores = (
        jnp.einsum("qhd,khd->hqk", query_heads, key_heads, preferred_element_type=jnp.float32)
        * score_scale
    )
    new_best = jnp.maximum(row_best, jnp.max(scores, axis=-1))
    exp_weights = jnp.exp(scores - new_best[..., None])
    running_sum = jnp.sum(exp_weights, axis=-1)
    weighted = jnp.einsum(
        "hqk,khd->hqd",
        exp_weights.astype(jnp.bfloat16),
        value_heads,
        preferred_element_type=jnp.float32,
    )
    row_best, running_sum, weighted = (new_best, running_sum, weighted)
    context = (
        (weighted / running_sum[..., None])
        .transpose(1, 0, 2)
        .reshape(row_count, col_count)
        .astype(jnp.bfloat16)
    )
    attended = project_out(context, attn_out_weight)
    share_cols = feature_share(attended)
    frame_cols = lax.dynamic_slice_in_dim(frames, column_start, col_count, 1)
    residual_cols = (frame_cols.astype(jnp.float32) + share_cols).astype(jnp.bfloat16)
    residual_full = lax.all_gather(residual_cols, "wt", axis=1, tiled=True)
    normed_conv = norm_rows(residual_full, conv_norm_gain)
    glu_pair = project_in(normed_conv, glu_weight)
    gated = (glu_pair[:, 0] * jax.nn.sigmoid(glu_pair[:, 1])).astype(jnp.bfloat16)
    rim_width = (depth_kernel.shape[0] - 1) // 2
    padded = padded_2(gated, (("seq", 0),), rim_width).astype(jnp.float32)
    depth_out = jnp.zeros((row_count, col_count), jnp.float32)
    for tap_index in range(depth_kernel.shape[0]):
        depth_out = depth_out + depth_kernel[tap_index] * padded[tap_index : tap_index + row_count]
    shifted = depth_out * norm_scale + norm_shift
    activated = (shifted * jax.nn.sigmoid(shifted)).astype(jnp.bfloat16)
    conv_cols = feature_share(project_out(activated, conv_out_weight))
    residual_cols = lax.dynamic_slice_in_dim(residual_full, column_start, col_count, 1)
    return (residual_cols.astype(jnp.float32) + conv_cols).astype(jnp.bfloat16)


def solution(mesh):
    in_specs = (
        P("seq", None),
        P(),
        P(None, "seq", "wt"),
        P("seq", "wt"),
        P(),
        P(None, "seq", "wt"),
        P(None, "wt"),
        P("wt"),
        P("wt"),
        P("seq", "wt"),
    )
    out_specs = P("seq", "wt")
    return jax.shard_map(local, mesh=mesh, in_specs=in_specs, out_specs=out_specs, check_vma=False)
```

profile of v0, /device:TPU:32, one launch (start us, length us, event | category | flops | bytes accessed | tf_op | source)
XLA Modules:
  0.0 819.5 jit_solution(16398674720940230616)
XLA Ops:
  6.5 0.0 copy-start.1
  6.5 0.0 copy-start.4
  6.5 0.0 all-gather.10.cloned.1.call-start
  6.5 2.1 copy.11
  8.6 0.0 all-gather.10.cloned.1.call-update
  8.6 0.0 all-gather.20.cloned.1.call-start
  8.7 2.0 convert_reduce_fusion.1
  10.7 0.0 copy-done.1
  10.7 0.7 fusion.9
  11.4 156.5 %all-gather.10.cloned.1.call-done = bf16[3,4096,256]{1,2,0:T(8,128)(2,1)} async-done(((bf16[3,256,256]{1,2,0:T(8,128)(2,1)}), bf16[3,4096,256]{1,2,0:T(8,128)(2,1)}) %all-gather.10.cloned.1.call-update) | async-done | bytes 6291472 | tf_op jit(solution)/shard_map/all_gather | solution.py:34
  167.9 0.0 copy-done.4
  167.9 4.7 fusion.28
  172.6 0.7 fusion.113
  173.3 0.0 all-gather.20.cloned.1.call-update
  173.4 0.0 all-gather.22.cloned.1.call-start
  173.4 0.7 all-gather.22.cloned.1.call-update
  174.1 0.0 all-gather.12.cloned.1.call-start
  174.1 0.5 all-gather.12.cloned.1.call-update
  174.7 0.0 reduce-scatter.3.cloned.1.call-start
  174.7 85.2 %all-gather.20.cloned.1.call-done = bf16[4096,1,256]{0,2,1:T(8,128)(2,1)} async-done(((bf16[256,1,256]{0,2,1:T(8,128)(2,1)}), bf16[4096,1,256]{0,2,1:T(8,128)(2,1)}) %all-gather.20.cloned.1.call-update) | async-done | bytes 2097168 | tf_op jit(solution)/shard_map/all_gather | solution.py:76
  260.0 3.0 multiply_reduce_fusion
  262.9 0.0 copy-start
  263.0 3.2 copy-done
  266.2 1.5 fusion
  267.7 77.6 %all-gather.22.cloned.1.call-done = bf16[4096,1,256]{0,2,1:T(8,128)(2,1)} async-done(((bf16[256,1,256]{0,2,1:T(8,128)(2,1)}), bf16[4096,1,256]{0,2,1:T(8,128)(2,1)}) %all-gather.22.cloned.1.call-update) | async-done | bytes 2097168 | tf_op jit(solution)/shard_map/all_gather | solution.py:77
  345.3 5.8 fusion.37
  351.1 0.0 copy-start.3
  351.1 69.0 %all-gather.12.cloned.1.call-done = bf16[4096,256]{1,0:T(8,128)(2,1)} async-done(((bf16[256,256]{1,0:T(8,128)(2,1)}), bf16[4096,256]{1,0:T(8,128)(2,1)}) %all-gather.12.cloned.1.call-update) | async-done | bytes 2097168 | tf_op jit(solution)/shard_map/all_gather | solution.py:42
  420.2 3.7 convolution_convert_fusion.1
  423.9 0.0 copy-start.5
  423.9 0.0 reduce-scatter.3.cloned.1.call-update
  423.9 0.0 all-gather.14.cloned.1.call-start
  423.9 77.6 %reduce-scatter.3.cloned.1.call-done = bf16[256,256]{1,0:T(8,128)(2,1)} async-done(((bf16[256,4096]{1,0:T(8,128)(2,1)}), bf16[256,256]{1,0:T(8,128)(2,1)}) %reduce-scatter.3.cloned.1.call-update) | async-done | bytes 131088 | tf_op jit(solution)/shard_map/reduce_scatter | solution.py:49
  501.5 1.6 add_convert_fusion.1
  503.1 0.0 all-gather.14.cloned.1.call-update
  503.1 0.0 all-gather.16.cloned.1.call-start
  503.2 0.7 all-gather.16.cloned.1.call-update
  503.9 0.0 all-gather.18.cloned.1.call-start
  503.9 0.7 all-gather.18.cloned.1.call-update
  504.6 0.0 reduce-scatter.5.cloned.1.call-start
  504.7 0.0 copy-done.3
  504.7 50.7 %all-gather.14.cloned.1.call-done = bf16[256,4096]{1,0:T(8,128)(2,1)} async-done(((bf16[256,256]{1,0:T(8,128)(2,1)}), bf16[256,4096]{1,0:T(8,128)(2,1)}) %all-gather.14.cloned.1.call-update) | async-done | bytes 2097168 | tf_op jit(solution)/shard_map/all_gather | solution.py:105
  555.5 0.0 copy-start.2
  555.5 2.1 convert_reduce_fusion
  557.6 2.3 fusion.6
  559.9 0.0 copy-start.6
  559.9 0.0 copy-start.7
  559.9 94.7 %all-gather.16.cloned.1.call-done = bf16[2,4096,256]{2,1,0:T(8,128)(2,1)} async-done(((bf16[2,256,256]{2,1,0:T(8,128)(2,1)}), bf16[2,4096,256]{2,1,0:T(8,128)(2,1)}) %all-gather.16.cloned.1.call-update) | async-done | bytes 4194320 | tf_op jit(solution)/shard_map/all_gather | solution.py:34
  654.6 0.0 copy-done.5
  654.6 0.0 copy-done.2
  654.6 3.5 fusion.20
  658.1 0.1 fusion.76
  658.2 3.9 collective-permute-start
  662.0 2.9 collective-permute-start.1
  664.9 0.1 fusion.124
  665.0 0.0 collective-permute-done
  665.0 2.6 collective-permute-done.1
  667.6 61.0 %all-gather.18.cloned.1.call-done = bf16[4096,256]{1,0:T(8,128)(2,1)} async-done(((bf16[256,256]{1,0:T(8,128)(2,1)}), bf16[4096,256]{1,0:T(8,128)(2,1)}) %all-gather.18.cloned.1.call-update) | async-done | bytes 2097168 | tf_op jit(solution)/shard_map/all_gather | solution.py:42
  728.6 0.0 copy-done.6
  728.6 0.0 copy-done.7
  728.6 4.6 convolution_convert_fusion
  733.2 0.0 reduce-scatter.5.cloned.1.call-update
  733.2 78.1 %reduce-scatter.5.cloned.1.call-done = bf16[256,256]{1,0:T(8,128)(2,1)} async-done(((bf16[256,4096]{1,0:T(8,128)(2,1)}), bf16[256,256]{1,0:T(8,128)(2,1)}) %reduce-scatter.5.cloned.1.call-update) | async-done | bytes 131088 | tf_op jit(solution)/shard_map/reduce_scatter | solution.py:49
  811.3 1.6 add_convert_fusion
  (9 shorter events, 0.1 us)
Async XLA Ops:
  6.5 4.1 copy-start.1
  6.5 161.3 %copy-start.4 = (f32[4096]{0:T(1024)S(1)}, f32[4096]{0:T(1024)}, u32[]{:S(2)}) copy-start(f32[4096]{0:T(1024)} %param.11) | copy-start | bytes 49156
  6.5 161.3 %all-gather.10.cloned.1.call-start = ((), (), s32[]{:S(2)}) async-start(), calls=%async_computation.2 | async-start | bytes 6684672 | tf_op jit(solution)/shard_map/all_gather | solution.py:34
  8.6 251.3 %all-gather.20.cloned.1.call-start = ((), (), s32[]{:S(2)}) async-start(), calls=%async_computation.9 | async-start | bytes 2228224 | tf_op jit(solution)/shard_map/all_gather | solution.py:76
  173.4 172.0 %all-gather.22.cloned.1.call-start = ((), (), s32[]{:S(2)}) async-start(), calls=%async_computation.10 | async-start | bytes 2228224 | tf_op jit(solution)/shard_map/all_gather | solution.py:77
  174.1 246.1 %all-gather.12.cloned.1.call-start = ((), (), s32[]{:S(2)}) async-start(), calls=%async_computation.3 | async-start | bytes 2228224 | tf_op jit(solution)/shard_map/all_gather | solution.py:42
  174.7 326.9 %reduce-scatter.3.cloned.1.call-start = ((), (), s32[]{:S(2)}) async-start(), calls=%async_computation.4 | async-start | bytes 2228224 | tf_op jit(solution)/shard_map/reduce_scatter | solution.py:49
  262.9 3.2 copy-start
  351.1 153.6 %copy-start.3 = (f32[31,256]{1,0:T(8,128)S(1)}, f32[31,256]{1,0:T(8,128)}, u32[]{:S(2)}) copy-start(f32[31,256]{1,0:T(8,128)} %param.16) | copy-start | bytes 95236
  423.9 230.7 %copy-start.5 = (f32[4096]{0:T(1024)S(1)}, f32[4096]{0:T(1024)}, u32[]{:S(2)}) copy-start(f32[4096]{0:T(1024)} %param.14) | copy-start | bytes 49156
  423.9 131.6 %all-gather.14.cloned.1.call-start = ((), (), s32[]{:S(2)}) async-start(), calls=%async_computation.5 | async-start | bytes 2228224 | tf_op jit(solution)/shard_map/all_gather | solution.py:105
  503.1 151.4 %all-gather.16.cloned.1.call-start = ((), (), s32[]{:S(2)}) async-start(), calls=%async_computation.6 | async-start | bytes 4456448 | tf_op jit(solution)/shard_map/all_gather | solution.py:34
  503.9 224.7 %all-gather.18.cloned.1.call-start = ((), (), s32[]{:S(2)}) async-start(), calls=%async_computation.7 | async-start | bytes 2228224 | tf_op jit(solution)/shard_map/all_gather | solution.py:42
  504.6 306.7 %reduce-scatter.5.cloned.1.call-start = ((), (), s32[]{:S(2)}) async-start(), calls=%async_computation.8 | async-start | bytes 2228224 | tf_op jit(solution)/shard_map/reduce_scatter | solution.py:49
  555.5 99.1 %copy-start.2 = (bf16[256,4096]{1,0:T(8,128)(2,1)S(1)}, bf16[256,4096]{1,0:T(8,128)(2,1)}, u32[]{:S(2)}) copy-start(bf16[256,4096]{1,0:T(8,128)(2,1)} %all-gather.14.cloned.1.call-done) | copy-start | bytes 6291460
  559.9 168.8 %copy-start.6 = (f32[256]{0:T(256)S(1)}, f32[256]{0:T(256)}, u32[]{:S(2)}) copy-start(f32[256]{0:T(256)} %param.18) | copy-start | bytes 3076
  559.9 168.7 %copy-start.7 = (f32[256]{0:T(256)S(1)}, f32[256]{0:T(256)}, u32[]{:S(2)}) copy-start(f32[256]{0:T(256)} %param.17) | copy-start | bytes 3076
  658.2 6.8 collective-permute-start
  662.0 5.5 collective-permute-start.1
Sparse Core Ops, SparseCore 0:
  9.1 158.7 all-gather.9
  173.5 86.4 all-gather.19
  261.7 83.6 all-gather.21
  347.0 73.1 all-gather.11
  424.2 77.2 reduce-scatter.2
  504.3 51.1 all-gather.13
  557.4 97.1 all-gather.15
  656.5 72.0 all-gather.17
  733.4 77.9 reduce-scatter.4
where the time goes:
time: 820 us; the launch traced here: 819 us
  waiting for transfers between devices  756 us (92%)
  matrix products  25.2 us (3%)
  between operations  13.4 us (2%)
  other arithmetic  11.9 us (1%)
    all_gather x2, waiting for transfers between devices, project_in(): lax.all_gather(stacked, 'seq', axis=1, tiled=True)  251 us
    reduce_scatter x2, waiting for transfers between devices, feature_share(): lax.psum_scatter(partial_sums.astype(jnp.bfloat16), 'wt', scatter_dimensi...  156 us
    all_gather x2, waiting for transfers between devices, project_out(): lax.all_gather(weight, 'seq', axis=0, tiled=True)  130 us
    all_gather x1, waiting for transfers between devices, local(): key_segment = lax.all_gather(keys, 'seq', axis=0, tiled=True)  85.2 us
    all_gather x1, waiting for transfers between devices, local(): value_segment = lax.all_gather(values, 'seq', axis=0, tiled=True)  77.6 us
    all_gather x1, waiting for transfers between devices, local(): residual_full = lax.all_gather(residual_cols, 'wt', axis=1, tiled=True)  50.7 us
  transfers between devices with their start and end apart: 11, of which 10 were waited for; matrix products, arithmetic and copies ran while one was open for 3% of the time, Pallas kernels for 0%

commit v1 on v0

--- a/solution.py
+++ b/solution.py
@@ -73,7 +73,9 @@
     keys = projected[:, 1]
     values = projected[:, 2]
     score_scale = HEAD_DIM ** (-0.5)
-    key_segment = lax.all_gather(keys, "seq", axis=0, tiled=True)
+    key_segment = jnp.concatenate(
+        lax.all_to_all(jnp.stack([keys] * lax.axis_size("seq")), "seq", 0, 0), axis=0
+    )
     value_segment = lax.all_gather(values, "seq", axis=0, tiled=True)
     row_best = jnp.full((heads_here, row_count), -1e30, jnp.float32)
     key_heads = key_segment.reshape(key_segment.shape[0], heads_here, HEAD_DIM)

time: 820 us -> 760 us (0.927)
  waiting for transfers between devices: 756 us -> 679 us
  local copies, waits for them, and re-layouts: 6.1 us -> 15.9 us
    all_gather x1 -> x0, waiting for transfers between devices: 85.2 us -> none  [local(): key_segment = lax.all_gather(keys, 'seq', axis=0, tiled=True)]
    all_to_all x0 -> x1, waiting for transfers between devices: none -> 49.5 us  [local(): lax.all_to_all(jnp.stack([keys] * lax.axis_size('seq')), 'seq', 0, 0)]
    all_gather x1, waiting for transfers between devices: 77.6 us -> 35.2 us  [local(): value_segment = lax.all_gather(values, 'seq', axis=0, tiled=True)]
  transfers between devices with their start and end apart: 11 -> 11, of which waited for: 10 -> 10; matrix products, arithmetic and copies ran while one was open for 3% -> 4% of each run, Pallas kernels for 0% -> 0%
where the time goes in v1:
time: 760 us; the launch traced here: 759 us
  waiting for transfers between devices  679 us (89%)
  matrix products  25.2 us (3%)
  local copies, waits for them, and re-layouts  15.9 us (2%)
  between operations  13.7 us (2%)
  starting transfers between devices  13.4 us (2%)
  other arithmetic  11.9 us (2%)
    all_gather x2, waiting for transfers between devices, project_in(): lax.all_gather(stacked, 'seq', axis=1, tiled=True)  251 us
    reduce_scatter x2, waiting for transfers between devices, feature_share(): lax.psum_scatter(partial_sums.astype(jnp.bfloat16), 'wt', scatter_dimensi...  156 us
    all_gather x2, waiting for transfers between devices, project_out(): lax.all_gather(weight, 'seq', axis=0, tiled=True)  133 us
    all_gather x1, waiting for transfers between devices, local(): residual_full = lax.all_gather(residual_cols, 'wt', axis=1, tiled=True)  50.7 us
    all_to_all x1, waiting for transfers between devices, local(): lax.all_to_all(jnp.stack([keys] * lax.axis_size('seq')), 'seq', 0, 0)  49.5 us
    all_gather x1, waiting for transfers between devices, local(): value_segment = lax.all_gather(values, 'seq', axis=0, tiled=True)  35.2 us
  transfers between devices with their start and end apart: 11, of which 10 were waited for; matrix products, arithmetic and copies ran while one was open for 4% of the time, Pallas kernels for 0%

profile of v1, /device:TPU:32, one launch (start us, length us, event | category | flops | bytes accessed | tf_op | source)
XLA Modules:
  0.0 759.3 jit_solution(1842699147005935059)
XLA Ops:
  6.5 0.0 copy-start.1
  6.5 0.0 copy-start.4
  6.5 0.0 all-gather.8.cloned.1.call-start
  6.5 2.1 copy.17
  8.6 0.0 all-gather.8.cloned.1.call-update
  8.7 0.0 all-gather.18.cloned.1.call-start
  8.7 2.0 convert_reduce_fusion.1
  10.7 0.0 copy-done.1
  10.7 0.7 fusion.9
  11.4 156.5 %all-gather.8.cloned.1.call-done = bf16[3,4096,256]{1,2,0:T(8,128)(2,1)} async-done(((bf16[3,256,256]{1,2,0:T(8,128)(2,1)}), bf16[3,4096,256]{1,2,0:T(8,128)(2,1)}) %all-gather.8.cloned.1.call-update) | async-done | bytes 6291472 | tf_op jit(solution)/shard_map/all_gather | solution.py:34
  167.9 0.0 copy-done.4
  167.9 4.7 fusion.28
  172.6 0.7 slice_bitcast_fusion
  173.3 0.0 all-gather.18.cloned.1.call-update
  173.3 1.5 stack.3
  174.8 6.2 all-to-all-start
  181.0 0.0 all-gather.10.cloned.1.call-start
  181.1 0.7 all-gather.10.cloned.1.call-update
  181.8 0.0 reduce-scatter.3.cloned.1.call-start
  181.8 49.5 %all-to-all-done = bf16[16,256,256]{1,2,0:T(8,128)(2,1)} async-done(((bf16[16,256,256]{1,2,0:T(8,128)(2,1)}), bf16[16,256,256]{1,2,0:T(8,128)(2,1)}, u32[]{:S(2)}, u32[]{:S(2)}) %all-to-all-start) | async-done | bytes 2097184 | tf_op jit(solution)/shard_map/all_to_all | solution.py:77
  231.3 4.1 copy.18
  235.4 4.2 reshape_reshape.3
  239.6 3.0 multiply_reduce_fusion
  242.6 0.0 copy-start
  242.7 3.2 copy-done
  245.9 1.5 fusion
  247.4 35.2 %all-gather.18.cloned.1.call-done = bf16[4096,1,256]{0,2,1:T(8,128)(2,1)} async-done(((bf16[256,1,256]{0,2,1:T(8,128)(2,1)}), bf16[4096,1,256]{0,2,1:T(8,128)(2,1)}) %all-gather.18.cloned.1.call-update) | async-done | bytes 2097168 | tf_op jit(solution)/shard_map/all_gather | solution.py:79
  282.6 5.8 fusion.37
  288.4 0.0 copy-start.3
  288.4 71.5 %all-gather.10.cloned.1.call-done = bf16[4096,256]{1,0:T(8,128)(2,1)} async-done(((bf16[256,256]{1,0:T(8,128)(2,1)}), bf16[4096,256]{1,0:T(8,128)(2,1)}) %all-gather.10.cloned.1.call-update) | async-done | bytes 2097168 | tf_op jit(solution)/shard_map/all_gather | solution.py:42
  359.9 3.7 convolution_convert_fusion.1
  363.6 0.0 reduce-scatter.3.cloned.1.call-update
  363.6 0.0 all-gather.12.cloned.1.call-start
  363.7 77.6 %reduce-scatter.3.cloned.1.call-done = bf16[256,256]{1,0:T(8,128)(2,1)} async-done(((bf16[256,4096]{1,0:T(8,128)(2,1)}), bf16[256,256]{1,0:T(8,128)(2,1)}) %reduce-scatter.3.cloned.1.call-update) | async-done | bytes 131088 | tf_op jit(solution)/shard_map/reduce_scatter | solution.py:49
  441.3 1.6 add_convert_fusion.1
  442.9 0.0 all-gather.12.cloned.1.call-update
  442.9 0.0 all-gather.14.cloned.1.call-start
  443.0 0.5 all-gather.14.cloned.1.call-update
  443.5 0.0 all-gather.16.cloned.1.call-start
  443.5 0.7 all-gather.16.cloned.1.call-update
  444.2 0.2 reduce-scatter.5.cloned.1.call-start
  444.5 0.0 copy-done.3
  444.5 50.7 %all-gather.12.cloned.1.call-done = bf16[256,4096]{1,0:T(8,128)(2,1)} async-done(((bf16[256,256]{1,0:T(8,128)(2,1)}), bf16[256,4096]{1,0:T(8,128)(2,1)}) %all-gather.12.cloned.1.call-update) | async-done | bytes 2097168 | tf_op jit(solution)/shard_map/all_gather | solution.py:107
  495.2 2.1 convert_reduce_fusion
  497.3 2.3 fusion.6
  499.6 0.0 copy-start.6
  499.6 0.0 copy-start.7
  499.6 94.5 %all-gather.14.cloned.1.call-done = bf16[2,4096,256]{2,1,0:T(8,128)(2,1)} async-done(((bf16[2,256,256]{2,1,0:T(8,128)(2,1)}), bf16[2,4096,256]{2,1,0:T(8,128)(2,1)}) %all-gather.14.cloned.1.call-update) | async-done | bytes 4194320 | tf_op jit(solution)/shard_map/all_gather | solution.py:34
  594.2 0.0 copy-done.5
  594.2 0.0 copy-done.2
  594.2 3.5 fusion.20
  597.6 0.1 fusion.76
  597.7 3.9 collective-permute-start
  601.6 2.9 collective-permute-start.1
  604.5 0.1 fusion.123
  604.6 0.0 collective-permute-done
  604.6 2.5 collective-permute-done.1
  607.2 61.0 %all-gather.16.cloned.1.call-done = bf16[4096,256]{1,0:T(8,128)(2,1)} async-done(((bf16[256,256]{1,0:T(8,128)(2,1)}), bf16[4096,256]{1,0:T(8,128)(2,1)}) %all-gather.16.cloned.1.call-update) | async-done | bytes 2097168 | tf_op jit(solution)/shard_map/all_gather | solution.py:42
  668.2 0.0 copy-done.6
  668.2 0.0 copy-done.7
  668.2 4.6 convolution_convert_fusion
  672.8 0.0 reduce-scatter.5.cloned.1.call-update
  672.8 78.1 %reduce-scatter.5.cloned.1.call-done = bf16[256,256]{1,0:T(8,128)(2,1)} async-done(((bf16[256,4096]{1,0:T(8,128)(2,1)}), bf16[256,256]{1,0:T(8,128)(2,1)}) %reduce-scatter.5.cloned.1.call-update) | async-done | bytes 131088 | tf_op jit(solution)/shard_map/reduce_scatter | solution.py:49
  750.9 1.6 add_convert_fusion
  (11 shorter events, 0.1 us)
Async XLA Ops:
  6.5 4.1 copy-start.1
  6.5 161.3 %copy-start.4 = (f32[4096]{0:T(1024)S(1)}, f32[4096]{0:T(1024)}, u32[]{:S(2)}) copy-start(f32[4096]{0:T(1024)} %param.11) | copy-start | bytes 49156
  6.5 161.3 %all-gather.8.cloned.1.call-start = ((), (), s32[]{:S(2)}) async-start(), calls=%async_computation.3 | async-start | bytes 6684672 | tf_op jit(solution)/shard_map/all_gather | solution.py:34
  8.7 274.0 %all-gather.18.cloned.1.call-start = ((), (), s32[]{:S(2)}) async-start(), calls=%async_computation.10 | async-start | bytes 2228224 | tf_op jit(solution)/shard_map/all_gather | solution.py:79
  174.8 56.5 %all-to-all-start = ((bf16[16,256,256]{1,2,0:T(8,128)(2,1)}), bf16[16,256,256]{1,2,0:T(8,128)(2,1)}, u32[]{:S(2)}, u32[]{:S(2)}) async-start(bf16[16,256,256]{1,2,0:T(8,128)(2,1)} %stack.3), calls=%async_computation | async-start | bytes 4194304 | tf_op jit(solution)/shard_map/all_to_all | solution.py:77
  181.0 178.9 %all-gather.10.cloned.1.call-start = ((), (), s32[]{:S(2)}) async-start(), calls=%async_computation.4 | async-start | bytes 2228224 | tf_op jit(solution)/shard_map/all_gather | solution.py:42
  181.8 259.5 %reduce-scatter.3.cloned.1.call-start = ((), (), s32[]{:S(2)}) async-start(), calls=%async_computation.5 | async-start | bytes 2228224 | tf_op jit(solution)/shard_map/reduce_scatter | solution.py:49
  242.6 3.2 copy-start
  288.4 156.1 %copy-start.3 = (f32[31,256]{1,0:T(8,128)S(1)}, f32[31,256]{1,0:T(8,128)}, u32[]{:S(2)}) copy-start(f32[31,256]{1,0:T(8,128)} %param.16) | copy-start | bytes 95236
  363.6 230.5 %copy-start.5 = (f32[4096]{0:T(1024)S(1)}, f32[4096]{0:T(1024)}, u32[]{:S(2)}) copy-start(f32[4096]{0:T(1024)} %param.14) | copy-start | bytes 49156
  363.6 131.6 %all-gather.12.cloned.1.call-start = ((), (), s32[]{:S(2)}) async-start(), calls=%async_computation.6 | async-start | bytes 2228224 | tf_op jit(solution)/shard_map/all_gather | solution.py:107
  442.9 151.2 %all-gather.14.cloned.1.call-start = ((), (), s32[]{:S(2)}) async-start(), calls=%async_computation.7 | async-start | bytes 4456448 | tf_op jit(solution)/shard_map/all_gather | solution.py:34
  443.5 224.7 %all-gather.16.cloned.1.call-start = ((), (), s32[]{:S(2)}) async-start(), calls=%async_computation.8 | async-start | bytes 2228224 | tf_op jit(solution)/shard_map/all_gather | solution.py:42
  444.2 306.7 %reduce-scatter.5.cloned.1.call-start = ((), (), s32[]{:S(2)}) async-start(), calls=%async_computation.9 | async-start | bytes 2228224 | tf_op jit(solution)/shard_map/reduce_scatter | solution.py:49
  495.2 99.0 %copy-start.2 = (bf16[256,4096]{1,0:T(8,128)(2,1)S(1)}, bf16[256,4096]{1,0:T(8,128)(2,1)}, u32[]{:S(2)}) copy-start(bf16[256,4096]{1,0:T(8,128)(2,1)} %all-gather.12.cloned.1.call-done) | copy-start | bytes 6291460
  499.6 168.6 %copy-start.6 = (f32[256]{0:T(256)S(1)}, f32[256]{0:T(256)}, u32[]{:S(2)}) copy-start(f32[256]{0:T(256)} %param.18) | copy-start | bytes 3076
  499.6 168.6 %copy-start.7 = (f32[256]{0:T(256)S(1)}, f32[256]{0:T(256)}, u32[]{:S(2)}) copy-start(f32[256]{0:T(256)} %param.17) | copy-start | bytes 3076
  597.7 6.8 collective-permute-start
  601.6 5.5 collective-permute-start.1
Sparse Core Ops, SparseCore 0:
  9.1 158.7 all-gather.7
  173.4 109.1 all-gather.17
  284.4 75.4 all-gather.9
  363.9 77.3 reduce-scatter.2
  444.0 51.1 all-gather.11
  497.0 97.1 all-gather.13
  596.1 72.0 all-gather.15
  673.0 77.8 reduce-scatter.4
